TPU v7x, 128 devices: a whole 4x4x4 slice. The times are simulated.
128 devices in a mesh: row: 8 (over z, core), col: 16 (over y, x).
Axes of the slice: x: 4, y: 4, z: 4, core: 2. Of those that a mesh axis runs over, the one named last changes fastest.
Arguments:
- density_blocks: bfloat16 [1024, 16, 128, 128], P(('row', 'col')), may hold values from -6 to 6
- hamilton_blocks: bfloat16 [1024, 16, 128, 128], P(('row', 'col')), may hold values from -0.25 to 0.25
- density_cols: int32 [1024, 16], replicated, may hold values from 0 to 1023, as said below
- hamilton_cols: int32 [1024, 16], replicated, may hold values from 0 to 1023, as said below
Outputs:
- product_blocks: bfloat16 [1024, 16, 128, 128], P(('row', 'col'))
Inputs may be any that keep to these rules, and one draw needn't show every extreme that they name: `density_cols`: row r lists 16 distinct block columns in increasing order, each within 24 of r, r itself among them. `hamilton_cols`: row r lists 16 distinct block columns in increasing order, each within 24 of r, r itself among them.
All inputs are finite; a program needn't handle non-finite values.
Results may differ from a plain program's by a relative error of at most 0.001.
Values may be sent and summed in bfloat16 or wider, within the bound.
A program may use at most 192 MiB of HBM per device.

v0:
```python
import jax
import jax.numpy as jnp
from jax import lax
from jax.sharding import PartitionSpec as P

W = 24


def passed_along(block, axis, distance):
    devices = range(lax.axis_size(axis))
    route = [(i - distance, i) for i in devices if i - distance in devices]
    return lax.ppermute(block, axis, route)


def per_device(density_blocks, hamilton_blocks, density_cols, hamilton_cols):
    rows_dev = density_blocks.shape[0]
    left_strip, right_strip = (
        lax.all_to_all(density_blocks, "row", split_axis=0, concat_axis=0, tiled=True),
        lax.all_to_all(hamilton_blocks, "row", split_axis=0, concat_axis=0, tiled=True),
    )
    reach_strips = -(-W // rows_dev)
    gathered = []
    for heading in (1, -1):
        current = right_strip
        pieces = []
        for distance in range(reach_strips):
            current = passed_along(current, ("row", "col"), heading)
            pieces.append(current)
        gathered.append(pieces)
    window = jnp.concatenate(gathered[0][::-1] + [right_strip] + gathered[1], axis=0)
    first_row = lax.axis_index(("row", "col")) * rows_dev
    window_start = first_row - reach_strips * rows_dev

    def one_row(operand):
        left_row, offset = operand
        left_list = lax.dynamic_index_in_dim(density_cols, first_row + offset, 0, keepdims=False)
        right_rows = jnp.take(window, left_list - window_start, axis=0)
        right_lists = jnp.take(hamilton_cols, left_list, axis=0)
        matches = right_lists[None, :, :] == left_list[:, None, None]
        products = jnp.einsum(
            "mab,mnbc->mnac", left_row, right_rows, preferred_element_type=jnp.float32
        )
        summed = jnp.einsum(
            "qmn,mnac->qac",
            matches.astype(jnp.float32),
            products,
            precision=lax.Precision.HIGHEST,
            preferred_element_type=jnp.float32,
        )
        return summed.astype(jnp.bfloat16)

    offsets = jnp.arange(rows_dev, dtype=jnp.int32)
    product_strip = lax.map(one_row, (left_strip, offsets))
    return lax.all_to_all(product_strip, "row", split_axis=0, concat_axis=0, tiled=True)


def solution(mesh):
    return jax.shard_map(
        per_device,
        mesh=mesh,
        in_specs=(
            P(("row", "col"), None, None, None),
            P(("row", "col"), None, None, None),
            P(),
            P(),
        ),
        out_specs=P(("row", "col"), None, None, None),
        check_vma=False,
    )
```

profile of v0, /device:TPU:64, one launch (start us, length us, event | category | flops | bytes accessed | tf_op | source)
XLA Modules:
  0.0 893.2 jit_solution(10763188648940189669)
XLA Ops:
  0.0 52.3 %all_to_all.15 = bf16[8,16,128,128]{3,2,1,0:T(8,128)(2,1)S(1)} all-to-all(bf16[8,16,128,128]{3,2,1,0:T(8,128)(2,1)} %param.7), channel_id=1, replica_groups=mesh['row'=8,'col'=16] {'row'}, dimensions={0} | all-to-all | bytes 8388608 | tf_op jit(solution)/shard_map/all_to_all | solution.py:19
  62.1 87.9 %collective-permute-done = bf16[8,16,128,128]{3,2,1,0:T(8,128)(2,1)S(1)} collective-permute-done((bf16[8,16,128,128]{3,2,1,0:T(8,128)(2,1)S(1)}, bf16[8,16,128,128]{3,2,1,0:T(8,128)(2,1)S(1)}, u32[]{:S(2)}, u32[]{:S(2)}) %collective-permute-start) | collective-permute-done | bytes 4194336 | tf_op jit(solution)/shard_map/ppermute | solution.py:12
  161.7 86.8 %collective-permute-done.1 = bf16[8,16,128,128]{3,2,1,0:T(8,128)(2,1)} collective-permute-done((bf16[8,16,128,128]{3,2,1,0:T(8,128)(2,1)S(1)}, bf16[8,16,128,128]{3,2,1,0:T(8,128)(2,1)}, u32[]{:S(2)}, u32[]{:S(2)}) %collective-permute-start.1) | collective-permute-done | bytes 4194336 | tf_op jit(solution)/shard_map/ppermute | solution.py:12
  264.7 83.2 %collective-permute-done.2 = bf16[8,16,128,128]{3,2,1,0:T(8,128)(2,1)} collective-permute-done((bf16[8,16,128,128]{3,2,1,0:T(8,128)(2,1)}, bf16[8,16,128,128]{3,2,1,0:T(8,128)(2,1)}, u32[]{:S(2)}, u32[]{:S(2)}) %collective-permute-start.2) | collective-permute-done | bytes 4194336 | tf_op jit(solution)/shard_map/ppermute | solution.py:12
  373.9 465.3 %while.10 = (s32[]{:T(128)}, bf16[8,16,128,128]{3,2,1,0:T(8,128)(2,1)}, s32[8]{0:T(128)S(1)}, s32[]{:T(128)}, s32[1024,16]{1,0:T(8,128)S(1)}, /*index=5*/s32[102...) while((s32[]{:T(128)}, ...), condition=%wide.region_1.2_spmd, body=%wide.region_0.1_spmd.sunk | while | flops 1883511424 | bytes 94387128 | solution.py:53
  375.2 14.2 %gather_fusion = bf16[16,16,128,128]{3,2,1,0:T(8,128)(2,1)} fusion(bf16[56,16,128,128]{3,2,1,0:T(8,128)(2,1)} %get-tuple-element.184, s32[1024]{0:T(1024)S(1)} %get-tuple-element.150), kind=kCustom, calls=%fused_computation.1.clone.1 | custom fusion | bytes 16777280 | tf_op jit(solution)/shard_map/while/body/eval_jaxpr/jit(_take)/gather | solution.py:37
  401.1 17.6 %copy.17 = f32[16,16,128,128]{2,1,0,3:T(8,128)} copy(f32[16,16,128,128]{3,2,1,0:T(8,128)} %fusion.37) | data formatting | bytes 33554432 | tf_op jit(solution)/shard_map/while/body/eval_jaxpr/mab,mnbc->mnac/dot_general | solution.py:40
  419.4 11.8 %fusion.38 = bf16[1,16,128,128]{3,1,2,0:T(8,128)(2,1)S(1)} fusion(f32[16,16,128,128]{2,1,0,3:T(8,128)} %copy.17, s32[16,16]{1,0:T(8,128)S(1)} %broadcast_select_fusion.2, s32[16]{0:T(128)S(1)} %bitcast.62), kind=kOutput, calls=%fused_computation.10.clone.1 | convolution fusion | flops 805572608 | bytes 17302592 | tf_op jit(solution)/shard_map/while/body/eval_jaxpr/qmn,mnac->qac/dot_general | solution.py:43
  433.3 14.2 %gather_fusion = bf16[16,16,128,128]{3,2,1,0:T(8,128)(2,1)} fusion(bf16[56,16,128,128]{3,2,1,0:T(8,128)(2,1)} %get-tuple-element.184, s32[1024]{0:T(1024)S(1)} %get-tuple-element.150), kind=kCustom, calls=%fused_computation.1.clone.1 | custom fusion | bytes 16777280 | tf_op jit(solution)/shard_map/while/body/eval_jaxpr/jit(_take)/gather | solution.py:37
  459.3 17.6 %copy.17 = f32[16,16,128,128]{2,1,0,3:T(8,128)} copy(f32[16,16,128,128]{3,2,1,0:T(8,128)} %fusion.37) | data formatting | bytes 33554432 | tf_op jit(solution)/shard_map/while/body/eval_jaxpr/mab,mnbc->mnac/dot_general | solution.py:40
  477.5 11.8 %fusion.38 = bf16[1,16,128,128]{3,1,2,0:T(8,128)(2,1)S(1)} fusion(f32[16,16,128,128]{2,1,0,3:T(8,128)} %copy.17, s32[16,16]{1,0:T(8,128)S(1)} %broadcast_select_fusion.2, s32[16]{0:T(128)S(1)} %bitcast.62), kind=kOutput, calls=%fused_computation.10.clone.1 | convolution fusion | flops 805572608 | bytes 17302592 | tf_op jit(solution)/shard_map/while/body/eval_jaxpr/qmn,mnac->qac/dot_general | solution.py:43
  491.5 14.2 %gather_fusion = bf16[16,16,128,128]{3,2,1,0:T(8,128)(2,1)} fusion(bf16[56,16,128,128]{3,2,1,0:T(8,128)(2,1)} %get-tuple-element.184, s32[1024]{0:T(1024)S(1)} %get-tuple-element.150), kind=kCustom, calls=%fused_computation.1.clone.1 | custom fusion | bytes 16777280 | tf_op jit(solution)/shard_map/while/body/eval_jaxpr/jit(_take)/gather | solution.py:37
  517.5 17.6 %copy.17 = f32[16,16,128,128]{2,1,0,3:T(8,128)} copy(f32[16,16,128,128]{3,2,1,0:T(8,128)} %fusion.37) | data formatting | bytes 33554432 | tf_op jit(solution)/shard_map/while/body/eval_jaxpr/mab,mnbc->mnac/dot_general | solution.py:40
  549.7 14.2 %gather_fusion = bf16[16,16,128,128]{3,2,1,0:T(8,128)(2,1)} fusion(bf16[56,16,128,128]{3,2,1,0:T(8,128)(2,1)} %get-tuple-element.184, s32[1024]{0:T(1024)S(1)} %get-tuple-element.150), kind=kCustom, calls=%fused_computation.1.clone.1 | custom fusion | bytes 16777280 | tf_op jit(solution)/shard_map/while/body/eval_jaxpr/jit(_take)/gather | solution.py:37
  575.6 17.6 %copy.17 = f32[16,16,128,128]{2,1,0,3:T(8,128)} copy(f32[16,16,128,128]{3,2,1,0:T(8,128)} %fusion.37) | data formatting | bytes 33554432 | tf_op jit(solution)/shard_map/while/body/eval_jaxpr/mab,mnbc->mnac/dot_general | solution.py:40
  607.8 14.2 %gather_fusion = bf16[16,16,128,128]{3,2,1,0:T(8,128)(2,1)} fusion(bf16[56,16,128,128]{3,2,1,0:T(8,128)(2,1)} %get-tuple-element.184, s32[1024]{0:T(1024)S(1)} %get-tuple-element.150), kind=kCustom, calls=%fused_computation.1.clone.1 | custom fusion | bytes 16777280 | tf_op jit(solution)/shard_map/while/body/eval_jaxpr/jit(_take)/gather | solution.py:37
  633.8 17.6 %copy.17 = f32[16,16,128,128]{2,1,0,3:T(8,128)} copy(f32[16,16,128,128]{3,2,1,0:T(8,128)} %fusion.37) | data formatting | bytes 33554432 | tf_op jit(solution)/shard_map/while/body/eval_jaxpr/mab,mnbc->mnac/dot_general | solution.py:40
  666.0 14.2 %gather_fusion = bf16[16,16,128,128]{3,2,1,0:T(8,128)(2,1)} fusion(bf16[56,16,128,128]{3,2,1,0:T(8,128)(2,1)} %get-tuple-element.184, s32[1024]{0:T(1024)S(1)} %get-tuple-element.150), kind=kCustom, calls=%fused_computation.1.clone.1 | custom fusion | bytes 16777280 | tf_op jit(solution)/shard_map/while/body/eval_jaxpr/jit(_take)/gather | solution.py:37
  691.9 17.6 %copy.17 = f32[16,16,128,128]{2,1,0,3:T(8,128)} copy(f32[16,16,128,128]{3,2,1,0:T(8,128)} %fusion.37) | data formatting | bytes 33554432 | tf_op jit(solution)/shard_map/while/body/eval_jaxpr/mab,mnbc->mnac/dot_general | solution.py:40
  724.1 14.2 %gather_fusion = bf16[16,16,128,128]{3,2,1,0:T(8,128)(2,1)} fusion(bf16[56,16,128,128]{3,2,1,0:T(8,128)(2,1)} %get-tuple-element.184, s32[1024]{0:T(1024)S(1)} %get-tuple-element.150), kind=kCustom, calls=%fused_computation.1.clone.1 | custom fusion | bytes 16777280 | tf_op jit(solution)/shard_map/while/body/eval_jaxpr/jit(_take)/gather | solution.py:37
  750.1 17.6 %copy.17 = f32[16,16,128,128]{2,1,0,3:T(8,128)} copy(f32[16,16,128,128]{3,2,1,0:T(8,128)} %fusion.37) | data formatting | bytes 33554432 | tf_op jit(solution)/shard_map/while/body/eval_jaxpr/mab,mnbc->mnac/dot_general | solution.py:40
  782.3 14.2 %gather_fusion = bf16[16,16,128,128]{3,2,1,0:T(8,128)(2,1)} fusion(bf16[56,16,128,128]{3,2,1,0:T(8,128)(2,1)} %get-tuple-element.184, s32[1024]{0:T(1024)S(1)} %get-tuple-element.150), kind=kCustom, calls=%fused_computation.1.clone.1 | custom fusion | bytes 16777280 | tf_op jit(solution)/shard_map/while/body/eval_jaxpr/jit(_take)/gather | solution.py:37
  808.2 17.6 %copy.17 = f32[16,16,128,128]{2,1,0,3:T(8,128)} copy(f32[16,16,128,128]{3,2,1,0:T(8,128)} %fusion.37) | data formatting | bytes 33554432 | tf_op jit(solution)/shard_map/while/body/eval_jaxpr/mab,mnbc->mnac/dot_general | solution.py:40
  839.2 52.0 %all_to_all.16 = bf16[8,16,128,128]{3,2,1,0:T(8,128)(2,1)S(1)} all-to-all(bf16[8,16,128,128]{3,2,1,0:T(8,128)(2,1)} %get-tuple-element.52), channel_id=1, replica_groups=mesh['row'=8,'col'=16] {'row'}, dimensions={0} | all-to-all | bytes 8388608 | tf_op jit(solution)/shard_map/all_to_all | solution.py:54
  (117 shorter events, 247.8 us)
Async XLA Ops:
  0.0 264.3 %copy-start.6 = (s32[1024,16]{0,1:T(8,128)S(1)}, s32[1024,16]{0,1:T(8,128)}, u32[]{:S(2)}) copy-start(s32[1024,16]{0,1:T(8,128)} %param.8) | copy-start | bytes 196612
  0.0 264.5 %copy-start.7 = (s32[1024,16]{0,1:T(8,128)S(1)}, s32[1024,16]{0,1:T(8,128)}, u32[]{:S(2)}) copy-start(s32[1024,16]{0,1:T(8,128)} %param.9) | copy-start | bytes 196612
  52.3 3.4 copy-start
  52.3 97.8 %collective-permute-start = (bf16[8,16,128,128]{3,2,1,0:T(8,128)(2,1)S(1)}, bf16[8,16,128,128]{3,2,1,0:T(8,128)(2,1)S(1)}, u32[]{:S(2)}, u32[]{:S(2)}) collective-permute-start(bf16[8,16,128,128]{3,2,1,0:T(8,128)(2,1)S(1)} %all_to_all.15), channel_id=1, source_target_pairs={{0,1},{1,2},{2,3},{3,4},{4,5},{5,6},{6,7},{7,8},{8,9},{9,10},{10,1... | collective-permute-start | bytes 12582920 | tf_op jit(solution)/shard_map/ppermute | solution.py:12
  55.7 96.3 %collective-permute-start.3 = (bf16[8,16,128,128]{3,2,1,0:T(8,128)(2,1)S(1)}, bf16[8,16,128,128]{3,2,1,0:T(8,128)(2,1)S(1)}, u32[]{:S(2)}, u32[]{:S(2)}) collective-permute-start(bf16[8,16,128,128]{3,2,1,0:T(8,128)(2,1)S(1)} %all_to_all.15), channel_id=1, source_target_pairs={{1,0},{2,1},{3,2},{4,3},{5,4},{6,5},{7,6},{8,7},{9,8},{10,9},{11,1... | collective-permute-start | bytes 12582920 | tf_op jit(solution)/shard_map/ppermute | solution.py:12
  150.0 100.7 %copy-start.4 = (bf16[8,16,128,128]{3,2,1,0:T(8,128)(2,1)}, bf16[8,16,128,128]{3,2,1,0:T(8,128)(2,1)S(1)}, u32[]{:S(2)}) copy-start(bf16[8,16,128,128]{3,2,1,0:T(8,128)(2,1)S(1)} %collective-permute-done) | copy-start | bytes 12582916
  150.0 98.5 %collective-permute-start.1 = (bf16[8,16,128,128]{3,2,1,0:T(8,128)(2,1)S(1)}, bf16[8,16,128,128]{3,2,1,0:T(8,128)(2,1)}, u32[]{:S(2)}, u32[]{:S(2)}) collective-permute-start(bf16[8,16,128,128]{3,2,1,0:T(8,128)(2,1)S(1)} %collective-permute-done), channel_id=1, source_target_pairs={{0,1},{1,2},{2,3},{3,4},{4,5},{5,6},{6,7},{7,8},{8,9},{9,10},{10,1... | collective-permute-start | bytes 12582920 | tf_op jit(solution)/shard_map/ppermute | solution.py:12
  152.0 1.9 copy-start.2
  153.9 96.8 %collective-permute-start.4 = (bf16[8,16,128,128]{3,2,1,0:T(8,128)(2,1)S(1)}, bf16[8,16,128,128]{3,2,1,0:T(8,128)(2,1)}, u32[]{:S(2)}, u32[]{:S(2)}) collective-permute-start(bf16[8,16,128,128]{3,2,1,0:T(8,128)(2,1)S(1)} %collective-permute-done.3), channel_id=1, source_target_pairs={{1,0},{2,1},{3,2},{4,3},{5,4},{6,5},{7,6},{8,7},{9,8},{10,9},{11,1... | collective-permute-start | bytes 12582920 | tf_op jit(solution)/shard_map/ppermute | solution.py:12
  248.5 99.3 %collective-permute-start.2 = (bf16[8,16,128,128]{3,2,1,0:T(8,128)(2,1)}, bf16[8,16,128,128]{3,2,1,0:T(8,128)(2,1)}, u32[]{:S(2)}, u32[]{:S(2)}) collective-permute-start(bf16[8,16,128,128]{3,2,1,0:T(8,128)(2,1)} %collective-permute-done.1), channel_id=1, source_target_pairs={{0,1},{1,2},{2,3},{3,4},{4,5},{5,6},{6,7},{7,8},{8,9},{9,10},{10,1... | collective-permute-start | bytes 12582920 | tf_op jit(solution)/shard_map/ppermute | solution.py:12
  250.7 118.5 %collective-permute-start.5 = (bf16[8,16,128,128]{3,2,1,0:T(8,128)(2,1)}, bf16[8,16,128,128]{3,2,1,0:T(8,128)(2,1)}, u32[]{:S(2)}, u32[]{:S(2)}) collective-permute-start(bf16[8,16,128,128]{3,2,1,0:T(8,128)(2,1)} %collective-permute-done.4), channel_id=1, source_target_pairs={{1,0},{2,1},{3,2},{4,3},{5,4},{6,5},{7,6},{8,7},{9,8},{10,9},{11,1... | collective-permute-start | bytes 12582920 | tf_op jit(solution)/shard_map/ppermute | solution.py:12
  258.9 115.1 %all-to-all-start.1 = ((bf16[8,16,128,128]{3,2,1,0:T(8,128)(2,1)}), bf16[8,16,128,128]{3,2,1,0:T(8,128)(2,1)}, u32[]{:S(2)}, u32[]{:S(2)}) async-start(bf16[8,16,128,128]{3,2,1,0:T(8,128)(2,1)} %param.6), calls=%async_computation.1 | async-start | bytes 8388608 | tf_op jit(solution)/shard_map/all_to_all | solution.py:18
  264.7 92.8 %copy-start.5 = (bf16[8,16,128,128]{3,2,1,0:T(8,128)(2,1)S(1)}, bf16[8,16,128,128]{3,2,1,0:T(8,128)(2,1)}, u32[]{:S(2)}) copy-start(bf16[8,16,128,128]{3,2,1,0:T(8,128)(2,1)} %copy-done.4) | copy-start | bytes 12582916
  352.6 7.4 copy-start.1
  357.5 4.7 copy-start.3
where the time goes:
time: 900 us; the launch traced here: 893 us
  local copies, waits for them, and re-layouts  302 us (34%)
  waiting for transfers between devices  258 us (29%)
  matrix products  188 us (21%)
  blocking collectives  104 us (12%)
  starting transfers between devices  35 us (4%)
    ppermute x6, waiting for transfers between devices, passed_along(): return lax.ppermute(block, axis, route)  258 us
    dot_general x8, local copies, waits for them, and re-layouts, one_row(): jnp.einsum('mab,mnbc->mnac', left_row, right_rows, preferred_element_type...  141 us
    gather x8, local copies, waits for them, and re-layouts, one_row(): right_rows = jnp.take(window, left_list - window_start, axis=0)  114 us
    dot_general x8, matrix products, one_row(): jnp.einsum('qmn,mnac->qac', matches.astype(jnp.float32), products, precis...  94.2 us
    dot_general x8, matrix products, one_row(): jnp.einsum('mab,mnbc->mnac', left_row, right_rows, preferred_element_type...  93.8 us
    all_to_all x1, blocking collectives, per_device(): lax.all_to_all(hamilton_blocks, 'row', split_axis=0, concat_axis=0, tiled...  52.3 us
    all_to_all x1, blocking collectives, per_device(): lax.all_to_all(product_strip, 'row', split_axis=0, concat_axis=0, tiled=T...  52 us
    ppermute x6, starting transfers between devices, passed_along(): return lax.ppermute(block, axis, route)  29.6 us
  transfers between devices with their start and end apart: 7, of which 4 were waited for; matrix products, arithmetic and copies ran while one was open for 3% of the time, Pallas kernels for 0%

commit v1 on v0

v1 whole, which is shorter than its diff:
```python
import functools

import jax
import jax.numpy as jnp
from jax import lax
from jax.experimental import pallas as pl
from jax.experimental.pallas import tpu as pltpu
from jax.sharding import PartitionSpec as P

W = 24
LIST = 16
ROWS = 8
WINDOW = 2 * W + ROWS
MESH = pl.DeviceIdType.MESH
OWN, SIB, PAIR, PAIRF, YA, YB, YBF, DIN, OUT = range(9)


class Place:
    def __init__(self):
        self.row = lax.axis_index("row")
        self.col = lax.axis_index("col")
        self.z, self.core = self.row // 2, self.row % 2
        self.y, self.x = self.col // 4, self.col % 4
        self.half = self.x // 2
        self.side = (self.x + self.half) % 2
        self.slot = self.side * 4 + self.z
        self.group = self.slot * 4 + self.y
        self.quarter = self.half * 2 + self.core
        self.start = self.group * 32 + self.quarter * 8

    def home(self, slot):
        side = slot // 4
        x = side + self.half * (3 - 2 * side)
        return ((slot % 4) * 2 + self.x % 2, self.y * 4 + x)

    def source(self, k):
        return (k, self.y * 4 + self.quarter)

    def member(self, group, core):
        slot = group // 4
        side = slot // 4
        x = side + self.half * (3 - 2 * side)
        return ((slot % 4) * 2 + core, (group % 4) * 4 + x)


def kernel(index_ref, d_ref, h_ref, out_ref, window, dbuf, obuf, send, recv):
    at = Place()
    row, core = at.row, at.core
    sibling = (at.row + 1 - 2 * core, at.col)
    pair = (at.row, at.y * 4 + 3 - at.x)
    heading = 1 - 2 * at.half
    facing = 2 * core - 1
    across = at.group + facing
    ahead = at.group + heading
    behind = at.group - heading
    has_across = (across >= 0) & (across < 32)
    has_ahead = (ahead >= 0) & (ahead < 32)
    has_behind = (behind >= 0) & (behind < 32)
    across_dev = at.member(across, 1 - core)
    ahead_dev = at.member(ahead, core)
    behind_dev = at.member(behind, core)
    stays = at.x % 2 == core

    barrier = pltpu.get_barrier_semaphore()

    def greet(dev):
        pl.semaphore_signal(barrier, inc=1, device_id=dev, device_id_type=MESH)

    def greet_slot(i, _):
        @pl.when(jnp.logical_not(stays & (i == at.slot)))
        def _():
            greet(at.home(i))

        @pl.when(jnp.logical_not(stays & (i == row)))
        def _():
            greet(at.source(i))

        return 0

    lax.fori_loop(0, 8, greet_slot, 0)
    greet(sibling)
    greet(pair)
    pl.when(has_across)(lambda: greet(across_dev))
    pl.when(has_ahead)(lambda: greet(ahead_dev))
    pl.when(has_behind)(lambda: greet(behind_dev))
    count = (
        18
        - 2 * stays.astype(jnp.int32)
        + has_across.astype(jnp.int32)
        + has_ahead.astype(jnp.int32)
        + has_behind.astype(jnp.int32)
    )
    pl.semaphore_wait(barrier, count)

    def rows(w):
        return window.at[pl.ds(w * LIST, LIST)]

    def remote(src, dst, kind, s, r, dev):
        return pltpu.make_async_remote_copy(
            src_ref=src,
            dst_ref=dst,
            send_sem=send.at[kind, s],
            recv_sem=recv.at[kind, r],
            device_id=dev,
            device_id_type=MESH,
        )

    own = W
    to_sib = own + 8 * facing
    at_pair = own + 16 * heading
    to_pair = own - 16 * heading
    pair_to_sib = own + 16 * heading + 8 * facing
    to_across = own - 24 * facing
    at_ahead = own - 16 * heading
    behind_to_sib = own - 16 * heading + 8 * facing

    def send_in(src_ref, dst, kind):
        def body(i, _):
            slot = (i + row) % 8
            local = stays & (slot == at.slot)

            @pl.when(local)
            def _():
                pltpu.make_async_copy(src_ref.at[slot], dst, recv.at[kind, row]).start()

            @pl.when(jnp.logical_not(local))
            def _():
                remote(src_ref.at[slot], dst, kind, slot, row, at.home(slot)).start()

            return 0

        lax.fori_loop(0, 8, body, 0)

    send_in(h_ref, rows(own + row), OWN)
    send_in(d_ref, dbuf.at[pl.ds(row * LIST, LIST)], DIN)

    def arrived(ref, kind, k):
        pltpu.make_async_copy(ref, ref, recv.at[kind, k]).wait()

    def step(j, _):
        @pl.when(j < 8)
        def _():
            k = (at.slot - j + 8) % 8
            here = rows(own + k)
            arrived(here, OWN, k)
            remote(here, rows(to_pair + k), PAIR, k, k, pair).start()

            @pl.when(has_across)
            def _():
                remote(here, rows(to_across + k), YA, k, k, across_dev).start()

            remote(here, rows(to_sib + k), SIB, k, k, sibling).start()

        @pl.when(j >= 1)
        def _():
            k = (at.slot - j + 9) % 8
            here = rows(at_pair + k)
            arrived(here, PAIR, k)

            @pl.when(has_ahead)
            def _():
                remote(here, rows(at_ahead + k), YB, k, k, ahead_dev).start()

            remote(here, rows(pair_to_sib + k), PAIRF, k, k, sibling).start()

        return 0

    lax.fori_loop(0, 9, step, 0)

    def hand_on(j, _):
        k = (at.slot - j + 8) % 8
        here = rows(at_ahead + k)
        arrived(here, YB, k)
        remote(here, rows(behind_to_sib + k), YBF, k, k, sibling).start()
        return 0

    @pl.when(has_behind)
    def _():
        lax.fori_loop(0, 8, hand_on, 0)

    zero = WINDOW * LIST
    window[zero] = jnp.zeros(window.shape[1:], window.dtype)

    def collect(k, _):
        one = rows(k)
        arrived(one, SIB, k)
        arrived(one, PAIRF, k)

        @pl.when(has_across)
        def _():
            arrived(one, YA, k)

        @pl.when(has_behind)
        def _():
            arrived(one, YBF, k)

        arrived(one, DIN, k)
        return 0

    lax.fori_loop(0, 8, collect, 0)

    def multiply(j, _):
        k = (row + j) % 8

        def columns(p, _):
            total = jnp.zeros((128, 256), jnp.float32)
            for m in range(0, LIST, 2):
                left = jnp.concatenate([dbuf[k * LIST + m], dbuf[k * LIST + m + 1]], axis=1)
                base = (k * LIST + m) * LIST + 2 * p
                upper = jnp.concatenate([window[index_ref[base]], window[index_ref[base + 1]]], axis=1)
                lower = jnp.concatenate(
                    [window[index_ref[base + LIST]], window[index_ref[base + LIST + 1]]], axis=1
                )
                right = jnp.concatenate([upper, lower], axis=0)
                total = total + jnp.dot(left, right, preferred_element_type=jnp.float32)
            obuf[k * LIST + 2 * p] = total[:, :128].astype(obuf.dtype)
            obuf[k * LIST + 2 * p + 1] = total[:, 128:].astype(obuf.dtype)
            return 0

        lax.fori_loop(0, LIST // 2, columns, 0)
        here = obuf.at[pl.ds(k * LIST, LIST)]
        local = stays & (k == row)

        @pl.when(local)
        def _():
            pltpu.make_async_copy(here, out_ref.at[at.slot], recv.at[OUT, at.slot]).start()

        @pl.when(jnp.logical_not(local))
        def _():
            remote(here, out_ref.at[at.slot], OUT, k, at.slot, at.source(k)).start()

        return 0

    lax.fori_loop(0, 8, multiply, 0)

    def finish(k, _):
        one = rows(k)

        def sent(kind):
            pltpu.make_async_copy(one, one, send.at[kind, k]).wait()

        @pl.when(jnp.logical_not(stays & (k == at.slot)))
        def _():
            sent(OWN)
            sent(DIN)

        sent(SIB)
        sent(PAIR)
        sent(PAIRF)
        pl.when(has_across)(lambda: sent(YA))
        pl.when(has_ahead)(lambda: sent(YB))
        pl.when(has_behind)(lambda: sent(YBF))

        @pl.when(jnp.logical_not(stays & (k == row)))
        def _():
            sent(OUT)

        arrived(out_ref.at[k], OUT, k)
        return 0

    lax.fori_loop(0, 8, finish, 0)


def match_index(density_cols, hamilton_cols):
    start = Place().start
    left = lax.dynamic_slice_in_dim(density_cols, start, ROWS, 0)
    right = jnp.take(hamilton_cols, left, axis=0)
    hit = right[:, :, None, :] == left[:, None, :, None]
    n = jnp.arange(LIST, dtype=jnp.int32)
    which = jnp.sum(jnp.where(hit, n, 0), axis=-1)
    block = (left - start + W)[:, :, None] * LIST + which
    return jnp.where(jnp.any(hit, axis=-1), block, WINDOW * LIST).reshape(-1).astype(jnp.int32)


def per_device(density_blocks, hamilton_blocks, density_cols, hamilton_cols):
    index = match_index(density_cols, hamilton_cols)
    block = density_blocks.shape[2:]
    kind = density_blocks.dtype
    return pl.pallas_call(
        kernel,
        out_shape=jax.ShapeDtypeStruct(density_blocks.shape, kind),
        in_specs=[
            pl.BlockSpec(memory_space=pltpu.SMEM),
            pl.BlockSpec(memory_space=pl.ANY),
            pl.BlockSpec(memory_space=pl.ANY),
        ],
        out_specs=pl.BlockSpec(memory_space=pl.ANY),
        scratch_shapes=[
            pltpu.VMEM((WINDOW * LIST + 1, *block), kind),
            pltpu.VMEM((ROWS * LIST, *block), kind),
            pltpu.VMEM((ROWS * LIST, *block), kind),
            pltpu.SemaphoreType.DMA((9, 8)),
            pltpu.SemaphoreType.DMA((9, 8)),
        ],
        compiler_params=pltpu.CompilerParams(
            collective_id=0, has_side_effects=True, vmem_limit_bytes=52 << 20
        ),
        name="block_product",
    )(index, density_blocks, hamilton_blocks)


def solution(mesh):
    return jax.shard_map(
        per_device,
        mesh=mesh,
        in_specs=(
            P(("row", "col"), None, None, None),
            P(("row", "col"), None, None, None),
            P(),
            P(),
        ),
        out_specs=P(("row", "col"), None, None, None),
        check_vma=False,
    )
```

time: 900 us -> 376 us (0.42)
  the two profiles are of different devices: /device:TPU:64 before, /device:TPU:29 now
where the time goes in v1:
time: 376 us
  Pallas kernels  363 us (97%)
  local copies, waits for them, and re-layouts  7.62 us (2%)
  other arithmetic  4.83 us (1%)
    pallas_call x1, Pallas kernels, per_device(): pl.pallas_call(kernel, out_shape=jax.ShapeDtypeStruct(density_blocks.shap...  363 us

profile of v1, /device:TPU:29, one launch (start us, length us, event | category | flops | bytes accessed | tf_op | source)
XLA Modules:
  0.0 375.8 jit_solution(627276420034274705)
XLA Ops:
  0.0 0.0 copy-start
  0.0 0.8 copy-done
  0.8 0.1 constant_dynamic-slice_fusion
  0.9 0.1 copy.17
  1.0 0.1 reshape.20
  1.1 1.0 copy.16
  2.1 0.7 gather_fusion
  2.8 0.1 broadcast_select_fusion
  2.9 2.3 compare_reduce_fusion
  5.2 2.3 fusion
  7.5 0.1 add_select_fusion
  7.6 0.1 select_n.64.index_ref
  7.7 363.3 %block_product.1 = bf16[8,16,128,128]{3,2,1,0:T(8,128)(2,1)} custom-call(s32[2048]{0:T(1024)S(1)} %select_n.64.index_ref, bf16[8,16,128,128]{3,2,1,0:T(8,128)(2,1)} %d_ref.1, bf16[8,16,128,128]{3,2,1,0:T(8,128)(2,1)} %h_ref.1), custom_call_target="tpu_custom_call" | custom-call | tf_op jit(solution)/shard_map/block_product/pallas_call | solution.py:279
  371.0 4.8 %copy.19 = bf16[8,16,128,128]{3,2,1,0:T(8,128)(2,1)} copy(bf16[8,16,128,128]{3,2,1,0:T(8,128)(2,1)} %block_product.1) | data formatting | bytes 8388608
  (3 shorter events, 0.0 us)
Async XLA Ops:
  0.0 0.8 copy-start

commit v2 on v1

--- a/solution.py
+++ b/solution.py
@@ -12,7 +12,8 @@
 ROWS = 8
 WINDOW = 2 * W + ROWS
 MESH = pl.DeviceIdType.MESH
-OWN, SIB, PAIR, PAIRF, YA, YB, YBF, DIN, OUT = range(9)
+OWN, SIB, PAIR, PAIRF, YA, YB, YBF, DIN, OUT, RA, RAF, RB, RBF = range(13)
+DETOUR = 2
 
 
 class Place:
@@ -43,7 +44,16 @@
         return ((slot % 4) * 2 + core, (group % 4) * 4 + x)
 
 
-def kernel(index_ref, d_ref, h_ref, out_ref, window, dbuf, obuf, send, recv):
+def turn(i):
+    i = i // 2
+    return i + (i // 2) * (1 - 2 * (i % 2))
+
+
+def arrival(z, j):
+    return ((z - turn(j) + 4) % 4) * 2 + j % 2
+
+
+def kernel(index_ref, d_ref, h_ref, out_ref, window, dbuf, obuf, rbuf, send, recv):
     at = Place()
     row, core = at.row, at.core
     sibling = (at.row + 1 - 2 * core, at.col)
@@ -60,6 +70,19 @@
     ahead_dev = at.member(ahead, core)
     behind_dev = at.member(behind, core)
     stays = at.x % 2 == core
+    seam_a = has_across & (at.y == 3 * core)
+    relay_a = (at.y == 3 - 3 * core) & (at.slot + facing >= 0) & (at.slot + facing < 8)
+    a_next = at.member(at.group + 4 * facing, 1 - core)
+    a_from = at.member(at.group - 3 * facing, core)
+    a_to = at.member(at.group + 3 * facing, core)
+    edge = at.y == 3 * (1 - at.half)
+    seam_b = has_ahead & edge
+    relay_b = edge & (at.slot - heading >= 0) & (at.slot - heading < 8)
+    b_next = at.member(at.group + 4 * heading, core)
+    b_last = at.member(at.group - 4 * heading, core)
+    b_to = at.member(at.group - 3 * heading, core)
+    from_b = at.member(at.group + 3 * heading, core)
+    seam_in = has_behind & (at.y == 3 * at.half)
 
     barrier = pltpu.get_barrier_semaphore()
 
@@ -80,13 +103,23 @@
     lax.fori_loop(0, 8, greet_slot, 0)
     greet(sibling)
     greet(pair)
-    pl.when(has_across)(lambda: greet(across_dev))
+    pl.when(has_across & jnp.logical_not(seam_a))(lambda: greet(across_dev))
+    pl.when(seam_a)(lambda: (greet(a_next), greet(a_from)) and None)
+    pl.when(relay_a)(lambda: (greet(a_next), greet(a_to)) and None)
+    pl.when(seam_b)(lambda: greet(b_next))
+    pl.when(seam_in)(lambda: greet(from_b))
+    pl.when(relay_b)(lambda: (greet(b_last), greet(b_to)) and None)
     pl.when(has_ahead)(lambda: greet(ahead_dev))
     pl.when(has_behind)(lambda: greet(behind_dev))
     count = (
         18
         - 2 * stays.astype(jnp.int32)
         + has_across.astype(jnp.int32)
+        + seam_a.astype(jnp.int32)
+        + 2 * relay_a.astype(jnp.int32)
+        + seam_b.astype(jnp.int32)
+        + seam_in.astype(jnp.int32)
+        + 2 * relay_b.astype(jnp.int32)
         + has_ahead.astype(jnp.int32)
         + has_behind.astype(jnp.int32)
     )
@@ -95,11 +128,11 @@
     def rows(w):
         return window.at[pl.ds(w * LIST, LIST)]
 
-    def remote(src, dst, kind, s, r, dev):
+    def remote(src, dst, kind, s, r, dev, sent=None):
         return pltpu.make_async_remote_copy(
             src_ref=src,
             dst_ref=dst,
-            send_sem=send.at[kind, s],
+            send_sem=send.at[kind if sent is None else sent, s],
             recv_sem=recv.at[kind, r],
             device_id=dev,
             device_id_type=MESH,
@@ -116,7 +149,7 @@
 
     def send_in(src_ref, dst, kind):
         def body(i, _):
-            slot = (i + row) % 8
+            slot = (at.side * (1 - 2 * (i % 2)) + i % 2) * 4 + (at.z + turn(i)) % 4
             local = stays & (slot == at.slot)
 
             @pl.when(local)
@@ -132,7 +165,9 @@
         lax.fori_loop(0, 8, body, 0)
 
     send_in(h_ref, rows(own + row), OWN)
-    send_in(d_ref, dbuf.at[pl.ds(row * LIST, LIST)], DIN)
+
+    def relayed(i):
+        return rbuf.at[pl.ds(i * LIST, LIST)]
 
     def arrived(ref, kind, k):
         pltpu.make_async_copy(ref, ref, recv.at[kind, k]).wait()
@@ -140,35 +175,60 @@
     def step(j, _):
         @pl.when(j < 8)
         def _():
-            k = (at.slot - j + 8) % 8
+            k = arrival(at.z, j)
             here = rows(own + k)
             arrived(here, OWN, k)
             remote(here, rows(to_pair + k), PAIR, k, k, pair).start()
 
-            @pl.when(has_across)
+            @pl.when(has_across & jnp.logical_not(seam_a))
             def _():
                 remote(here, rows(to_across + k), YA, k, k, across_dev).start()
 
+            @pl.when(seam_a)
+            def _():
+                remote(here, relayed(k), RA, k, k, a_next, YA).start()
+
             remote(here, rows(to_sib + k), SIB, k, k, sibling).start()
 
         @pl.when(j >= 1)
         def _():
-            k = (at.slot - j + 9) % 8
+            k = arrival(at.z, j - 1)
             here = rows(at_pair + k)
             arrived(here, PAIR, k)
 
-            @pl.when(has_ahead)
+            around = seam_b & (j - 1 < DETOUR)
+
+            @pl.when(has_ahead & jnp.logical_not(around))
             def _():
                 remote(here, rows(at_ahead + k), YB, k, k, ahead_dev).start()
 
+            @pl.when(around)
+            def _():
+                remote(here, relayed(7 + j), RB, k, k, b_next, YB).start()
+
             remote(here, rows(pair_to_sib + k), PAIRF, k, k, sibling).start()
 
+        @pl.when((j >= 1) & relay_a)
+        def _():
+            k = arrival((at.z + facing + 4) % 4, j - 1)
+            here = relayed(k)
+            arrived(here, RA, k)
+            remote(here, rows(own + 24 * facing + k), YA, k, k, a_to, RAF).start()
+
+        @pl.when((j >= 2) & (j < 2 + DETOUR) & relay_b)
+        def _():
+            k = arrival((at.z - heading + 4) % 4, j - 2)
+            here = relayed(6 + j)
+            arrived(here, RB, k)
+            remote(here, rows(at_ahead + k), YB, k, k, b_to, RBF).start()
+
         return 0
 
     lax.fori_loop(0, 9, step, 0)
+    send_in(d_ref, dbuf.at[pl.ds(row * LIST, LIST)], DIN)
 
     def hand_on(j, _):
-        k = (at.slot - j + 8) % 8
+        k = arrival((behind // 4) % 4, j)
         here = rows(at_ahead + k)
         arrived(here, YB, k)
         remote(here, rows(behind_to_sib + k), YBF, k, k, sibling).start()
@@ -250,6 +310,12 @@
         pl.when(has_across)(lambda: sent(YA))
         pl.when(has_ahead)(lambda: sent(YB))
         pl.when(has_behind)(lambda: sent(YBF))
+        pl.when(relay_a)(lambda: sent(RAF))
+
+        @pl.when(relay_b & ((k == arrival((at.z - heading + 4) % 4, 0)) | (k == arrival((at.z - heading + 4) % 4, 1))))
+        def _():
+            sent(RBF)
+
 
         @pl.when(jnp.logical_not(stays & (k == row)))
         def _():
@@ -289,8 +355,9 @@
             pltpu.VMEM((WINDOW * LIST + 1, *block), kind),
             pltpu.VMEM((ROWS * LIST, *block), kind),
             pltpu.VMEM((ROWS * LIST, *block), kind),
-            pltpu.SemaphoreType.DMA((9, 8)),
-            pltpu.SemaphoreType.DMA((9, 8)),
+            pltpu.VMEM(((ROWS + DETOUR) * LIST, *block), kind),
+            pltpu.SemaphoreType.DMA((13, 8)),
+            pltpu.SemaphoreType.DMA((13, 8)),
         ],
         compiler_params=pltpu.CompilerParams(
             collective_id=0, has_side_effects=True, vmem_limit_bytes=52 << 20

time: 376 us -> 329 us (0.88)
  the two profiles are of different devices: /device:TPU:29 before, /device:TPU:25 now
where the time goes in v2:
time: 329 us
  Pallas kernels  316 us (96%)
  local copies, waits for them, and re-layouts  7.62 us (2%)
  other arithmetic  4.83 us (1%)
    pallas_call x1, Pallas kernels, per_device(): pl.pallas_call(kernel, out_shape=jax.ShapeDtypeStruct(density_blocks.shap...  316 us
    unnamed x5, local copies, waits for them, and re-layouts  6.74 us

profile of v2, /device:TPU:25, one launch (start us, length us, event | category | flops | bytes accessed | tf_op | source)
XLA Modules:
  0.0 328.9 jit_solution(4516550998437299507)
XLA Ops:
  0.0 0.0 copy-start
  0.0 0.8 copy-done
  0.8 0.1 constant_dynamic-slice_fusion
  0.9 0.1 copy.17
  1.0 0.1 reshape.20
  1.1 1.0 copy.16
  2.1 0.6 gather_fusion
  2.8 0.1 broadcast_select_fusion
  2.9 2.3 compare_reduce_fusion
  5.2 2.3 fusion
  7.5 0.1 add_select_fusion
  7.6 0.1 select_n.64.index_ref
  7.7 316.4 %block_product.1 = bf16[8,16,128,128]{3,2,1,0:T(8,128)(2,1)} custom-call(s32[2048]{0:T(1024)S(1)} %select_n.64.index_ref, bf16[8,16,128,128]{3,2,1,0:T(8,128)(2,1)} %d_ref.1, bf16[8,16,128,128]{3,2,1,0:T(8,128)(2,1)} %h_ref.1), custom_call_target="tpu_custom_call" | custom-call | tf_op jit(solution)/shard_map/block_product/pallas_call | solution.py:345
  324.1 4.8 %copy.19 = bf16[8,16,128,128]{3,2,1,0:T(8,128)(2,1)} copy(bf16[8,16,128,128]{3,2,1,0:T(8,128)(2,1)} %block_product.1) | data formatting | bytes 8388608
  (3 shorter events, 0.0 us)
Async XLA Ops:
  0.0 0.8 copy-start

commit v3 on v2

--- a/solution.py
+++ b/solution.py
@@ -12,8 +12,20 @@
 ROWS = 8
 WINDOW = 2 * W + ROWS
 MESH = pl.DeviceIdType.MESH
-OWN, SIB, PAIR, PAIRF, YA, YB, YBF, DIN, OUT, RA, RAF, RB, RBF = range(13)
+OWN, SIB, PAIR, PAIRF, YA, YB, YBF, DIN, OUT, RA, RAF, RB, RBF, YP, YPF = range(15)
 DETOUR = 2
+A_DELAY = 8
+D_START = 4
+STEPS = 19
+
+
+def ring(side, i):
+    return side * 3 + i * (1 - 2 * side)
+
+
+def ring_of(group):
+    slot = group // 4
+    return ring(slot // 4, slot % 4)
 
 
 class Place:
@@ -24,7 +36,7 @@
         self.y, self.x = self.col // 4, self.col % 4
         self.half = self.x // 2
         self.side = (self.x + self.half) % 2
-        self.slot = self.side * 4 + self.z
+        self.slot = self.side * 4 + ring(self.side, self.z)
         self.group = self.slot * 4 + self.y
         self.quarter = self.half * 2 + self.core
         self.start = self.group * 32 + self.quarter * 8
@@ -32,7 +44,7 @@
     def home(self, slot):
         side = slot // 4
         x = side + self.half * (3 - 2 * side)
-        return ((slot % 4) * 2 + self.x % 2, self.y * 4 + x)
+        return (ring(side, slot % 4) * 2 + self.x % 2, self.y * 4 + x)
 
     def source(self, k):
         return (k, self.y * 4 + self.quarter)
@@ -41,7 +53,7 @@
         slot = group // 4
         side = slot // 4
         x = side + self.half * (3 - 2 * side)
-        return ((slot % 4) * 2 + core, (group % 4) * 4 + x)
+        return (ring(side, slot % 4) * 2 + core, (group % 4) * 4 + x)
 
 
 def turn(i):
@@ -70,19 +82,41 @@
     ahead_dev = at.member(ahead, core)
     behind_dev = at.member(behind, core)
     stays = at.x % 2 == core
+    def near(slot):
+        return (slot >= 0) & (slot < 8)
+
+    def flips(slot):
+        return at.slot + slot == 7
+
+    def pick(cond, a, b):
+        return jnp.where(cond, a, b)
+
     seam_a = has_across & (at.y == 3 * core)
-    relay_a = (at.y == 3 - 3 * core) & (at.slot + facing >= 0) & (at.slot + facing < 8)
-    a_next = at.member(at.group + 4 * facing, 1 - core)
-    a_from = at.member(at.group - 3 * facing, core)
-    a_to = at.member(at.group + 3 * facing, core)
-    edge = at.y == 3 * (1 - at.half)
-    seam_b = has_ahead & edge
-    relay_b = edge & (at.slot - heading >= 0) & (at.slot - heading < 8)
-    b_next = at.member(at.group + 4 * heading, core)
-    b_last = at.member(at.group - 4 * heading, core)
-    b_to = at.member(at.group - 3 * heading, core)
-    from_b = at.member(at.group + 3 * heading, core)
-    seam_in = has_behind & (at.y == 3 * at.half)
+    flip_a = flips(at.slot + facing)
+    a_next = at.member(at.group + pick(flip_a, -3 * facing, 4 * facing), 1 - core)
+    a_from = at.member(at.group + pick(flip_a, 4 * facing, -3 * facing), core)
+    turn_a = (at.y == 3 * core) & flips(at.slot - facing)
+    relay_a = turn_a | (
+        (at.y == 3 - 3 * core) & near(at.slot + facing) & jnp.logical_not(flip_a)
+    )
+    a_group = at.group + pick(turn_a, -3 * facing, 4 * facing)
+    a_last = at.member(a_group, 1 - core)
+    a_to = at.member(at.group + pick(turn_a, -4 * facing, 3 * facing), core)
+    outer = core == at.half
+    inner = core != at.half
+    seam_b = has_ahead & outer & (at.y == 3 - 3 * at.half)
+    seam_in = has_behind & outer & (at.y == 3 * at.half)
+    flip_ahead = flips(at.slot + heading)
+    flip_behind = flips(at.slot - heading)
+    b_next = at.member(at.group + pick(flip_ahead, -3 * heading, 4 * heading), core)
+    from_b = at.member(at.group + pick(flip_behind, -4 * heading, 3 * heading), core)
+    turn_b = outer & (at.y == 3 * at.half) & flip_ahead
+    relay_b = turn_b | (
+        outer & (at.y == 3 - 3 * at.half) & near(at.slot - heading) & jnp.logical_not(flip_behind)
+    )
+    b_group = at.group + pick(turn_b, 3 * heading, -4 * heading)
+    b_last = at.member(b_group, core)
+    b_to = at.member(at.group + pick(turn_b, 4 * heading, -3 * heading), core)
 
     barrier = pltpu.get_barrier_semaphore()
 
@@ -105,7 +139,7 @@
     greet(pair)
     pl.when(has_across & jnp.logical_not(seam_a))(lambda: greet(across_dev))
     pl.when(seam_a)(lambda: (greet(a_next), greet(a_from)) and None)
-    pl.when(relay_a)(lambda: (greet(a_next), greet(a_to)) and None)
+    pl.when(relay_a)(lambda: (greet(a_last), greet(a_to)) and None)
     pl.when(seam_b)(lambda: greet(b_next))
     pl.when(seam_in)(lambda: greet(from_b))
     pl.when(relay_b)(lambda: (greet(b_last), greet(b_to)) and None)
@@ -146,25 +180,27 @@
     to_across = own - 24 * facing
     at_ahead = own - 16 * heading
     behind_to_sib = own - 16 * heading + 8 * facing
-
-    def send_in(src_ref, dst, kind):
-        def body(i, _):
-            slot = (at.side * (1 - 2 * (i % 2)) + i % 2) * 4 + (at.z + turn(i)) % 4
-            local = stays & (slot == at.slot)
-
-            @pl.when(local)
-            def _():
-                pltpu.make_async_copy(src_ref.at[slot], dst, recv.at[kind, row]).start()
-
-            @pl.when(jnp.logical_not(local))
-            def _():
-                remote(src_ref.at[slot], dst, kind, slot, row, at.home(slot)).start()
-
-            return 0
-
-        lax.fori_loop(0, 8, body, 0)
-
-    send_in(h_ref, rows(own + row), OWN)
+    across_to_pair = own + 24 * facing - 16 * heading
+    from_pair = own - 16 * heading - 8 * facing
+
+    def send_home(src_ref, dst, kind, i):
+        side = at.side * (1 - 2 * (i % 2)) + i % 2
+        slot = side * 4 + ring(side, (at.z + turn(i)) % 4)
+        local = stays & (slot == at.slot)
+
+        @pl.when(local)
+        def _():
+            pltpu.make_async_copy(src_ref.at[slot], dst, recv.at[kind, row]).start()
+
+        @pl.when(jnp.logical_not(local))
+        def _():
+            remote(src_ref.at[slot], dst, kind, slot, row, at.home(slot)).start()
+
+    def send_h(i, _):
+        send_home(h_ref, rows(own + row), OWN, i)
+        return 0
+
+    lax.fori_loop(0, 8, send_h, 0)
 
     def relayed(i):
         return rbuf.at[pl.ds(i * LIST, LIST)]
@@ -172,10 +208,10 @@
     def arrived(ref, kind, k):
         pltpu.make_async_copy(ref, ref, recv.at[kind, k]).wait()
 
-    def step(j, _):
-        @pl.when(j < 8)
-        def _():
-            k = arrival(at.z, j)
+    def step(u, _):
+        @pl.when(u < 8)
+        def _():
+            k = arrival(at.z, u)
             here = rows(own + k)
             arrived(here, OWN, k)
             remote(here, rows(to_pair + k), PAIR, k, k, pair).start()
@@ -184,54 +220,87 @@
             def _():
                 remote(here, rows(to_across + k), YA, k, k, across_dev).start()
 
-            @pl.when(seam_a)
-            def _():
-                remote(here, relayed(k), RA, k, k, a_next, YA).start()
-
             remote(here, rows(to_sib + k), SIB, k, k, sibling).start()
 
-        @pl.when(j >= 1)
-        def _():
-            k = arrival(at.z, j - 1)
+        @pl.when((u >= 3) & (u < 18) & (u % 2 == 1))
+        def _():
+            j = (u - 3) // 2
+            k = arrival(at.z, j)
             here = rows(at_pair + k)
             arrived(here, PAIR, k)
-
-            around = seam_b & (j - 1 < DETOUR)
-
-            @pl.when(has_ahead & jnp.logical_not(around))
+            around = seam_b & (j < DETOUR)
+
+            @pl.when(has_ahead & (outer | (k % 2 == 0)) & jnp.logical_not(around))
             def _():
                 remote(here, rows(at_ahead + k), YB, k, k, ahead_dev).start()
 
             @pl.when(around)
             def _():
-                remote(here, relayed(7 + j), RB, k, k, b_next, YB).start()
+                remote(here, relayed(8 + j), RB, k, k, b_next, YB).start()
 
             remote(here, rows(pair_to_sib + k), PAIRF, k, k, sibling).start()
 
-        @pl.when((j >= 1) & relay_a)
-        def _():
-            k = arrival((at.z + facing + 4) % 4, j - 1)
+        @pl.when((u >= A_DELAY) & (u < A_DELAY + 8) & seam_a)
+        def _():
+            k = arrival(at.z, u - A_DELAY)
+            remote(rows(own + k), relayed(k), RA, k, k, a_next, YA).start()
+
+        @pl.when((u >= A_DELAY + 3) & (u < A_DELAY + 11) & relay_a)
+        def _():
+            k = arrival(ring_of(a_group), u - A_DELAY - 3)
             here = relayed(k)
             arrived(here, RA, k)
             remote(here, rows(own + 24 * facing + k), YA, k, k, a_to, RAF).start()
 
-        @pl.when((j >= 2) & (j < 2 + DETOUR) & relay_b)
-        def _():
-            k = arrival((at.z - heading + 4) % 4, j - 2)
-            here = relayed(6 + j)
+        @pl.when((u == 7) & relay_b | (u == 9) & relay_b)
+        def _():
+            j = (u - 7) // 2
+            k = arrival(ring_of(b_group), j)
+            here = relayed(8 + j)
             arrived(here, RB, k)
             remote(here, rows(at_ahead + k), YB, k, k, b_to, RBF).start()
 
-        return 0
-
-    lax.fori_loop(0, 9, step, 0)
-    send_in(d_ref, dbuf.at[pl.ds(row * LIST, LIST)], DIN)
+        @pl.when((u >= 10) & (u < 18) & (u % 2 == 0) & inner & has_across & jnp.logical_not(seam_a))
+        def _():
+            across_on(u - 9)
+
+        @pl.when((u >= D_START) & (u < D_START + 8))
+        def _():
+            send_home(d_ref, dbuf.at[pl.ds(row * LIST, LIST)], DIN, u - D_START)
+
+        return 0
+
+    def across_on(i):
+        k = arrival(ring_of(across), i)
+        here = rows(own + 24 * facing + k)
+        arrived(here, YA, k)
+        remote(here, rows(across_to_pair + k), YBF, k, k, pair, YP).start()
+
+    lax.fori_loop(0, STEPS, step, 0)
+
+    @pl.when(inner & seam_a)
+    def _():
+        def body(i, _):
+            across_on(2 * i + 1)
+            return 0
+
+        lax.fori_loop(0, 4, body, 0)
 
     def hand_on(j, _):
-        k = arrival((behind // 4) % 4, j)
-        here = rows(at_ahead + k)
-        arrived(here, YB, k)
-        remote(here, rows(behind_to_sib + k), YBF, k, k, sibling).start()
+        k = arrival(ring_of(behind), j)
+
+        @pl.when(outer | (k % 2 == 0))
+        def _():
+            here = rows(at_ahead + k)
+            arrived(here, YB, k)
+            remote(here, rows(behind_to_sib + k), YBF, k, k, sibling).start()
+
+        @pl.when(outer & (k % 2 == 1))
+        def _():
+            here = rows(from_pair + k)
+            arrived(here, YBF, k)
+            remote(here, rows(at_ahead + k), YB, k, k, sibling, YPF).start()
+
         return 0
 
     @pl.when(has_behind)
@@ -246,21 +315,25 @@
         arrived(one, SIB, k)
         arrived(one, PAIRF, k)
 
-        @pl.when(has_across)
+        @pl.when(has_across & (outer | (k % 2 == 0)))
         def _():
             arrived(one, YA, k)
 
-        @pl.when(has_behind)
+        @pl.when(has_behind & (inner | (k % 2 == 0)))
         def _():
             arrived(one, YBF, k)
 
+        @pl.when(has_behind & inner & (k % 2 == 1))
+        def _():
+            arrived(one, YB, k)
+
         arrived(one, DIN, k)
         return 0
 
     lax.fori_loop(0, 8, collect, 0)
 
     def multiply(j, _):
-        k = (row + j) % 8
+        k = arrival(at.z, 7 - j)
 
         def columns(p, _):
             total = jnp.zeros((128, 256), jnp.float32)
@@ -308,11 +381,13 @@
         sent(PAIR)
         sent(PAIRF)
         pl.when(has_across)(lambda: sent(YA))
-        pl.when(has_ahead)(lambda: sent(YB))
-        pl.when(has_behind)(lambda: sent(YBF))
+        pl.when(has_ahead & (outer | (k % 2 == 0)))(lambda: sent(YB))
+        pl.when(has_behind & (outer | (k % 2 == 0)))(lambda: sent(YBF))
+        pl.when(has_across & inner & (k % 2 == 1))(lambda: sent(YP))
+        pl.when(has_behind & outer & (k % 2 == 1))(lambda: sent(YPF))
         pl.when(relay_a)(lambda: sent(RAF))
 
-        @pl.when(relay_b & ((k == arrival((at.z - heading + 4) % 4, 0)) | (k == arrival((at.z - heading + 4) % 4, 1))))
+        @pl.when(relay_b & ((k == arrival(ring_of(b_group), 0)) | (k == arrival(ring_of(b_group), 1))))
         def _():
             sent(RBF)
 
@@ -356,8 +431,8 @@
             pltpu.VMEM((ROWS * LIST, *block), kind),
             pltpu.VMEM((ROWS * LIST, *block), kind),
             pltpu.VMEM(((ROWS + DETOUR) * LIST, *block), kind),
-            pltpu.SemaphoreType.DMA((13, 8)),
-            pltpu.SemaphoreType.DMA((13, 8)),
+            pltpu.SemaphoreType.DMA((15, 8)),
+            pltpu.SemaphoreType.DMA((15, 8)),
         ],
         compiler_params=pltpu.CompilerParams(
             collective_id=0, has_side_effects=True, vmem_limit_bytes=52 << 20

time: 329 us -> 261 us (0.79)
  the two profiles are of different devices: /device:TPU:25 before, /device:TPU:64 now
where the time goes in v3:
time: 261 us
  Pallas kernels  249 us (95%)
  local copies, waits for them, and re-layouts  7.62 us (3%)
  other arithmetic  4.83 us (2%)
    pallas_call x1, Pallas kernels, per_device(): pl.pallas_call(kernel, out_shape=jax.ShapeDtypeStruct(density_blocks.shap...  249 us
    unnamed x5, local copies, waits for them, and re-layouts  6.74 us

profile of v3, /device:TPU:64, one launch (start us, length us, event | category | flops | bytes accessed | tf_op | source)
XLA Modules:
  0.0 261.2 jit_solution(12045551873756642854)
XLA Ops:
  0.0 0.0 copy-start
  0.0 0.8 copy-done
  0.8 0.1 constant_dynamic-slice_fusion
  0.9 0.1 copy.17
  1.0 0.1 reshape.20
  1.1 1.0 copy.16
  2.1 0.6 gather_fusion
  2.8 0.1 broadcast_select_fusion
  2.9 2.3 compare_reduce_fusion
  5.2 2.3 fusion
  7.5 0.1 add_select_fusion
  7.6 0.1 select_n.64.index_ref
  7.7 248.7 %block_product.1 = bf16[8,16,128,128]{3,2,1,0:T(8,128)(2,1)} custom-call(s32[2048]{0:T(1024)S(1)} %select_n.64.index_ref, bf16[8,16,128,128]{3,2,1,0:T(8,128)(2,1)} %d_ref.1, bf16[8,16,128,128]{3,2,1,0:T(8,128)(2,1)} %h_ref.1), custom_call_target="tpu_custom_call" | custom-call | tf_op jit(solution)/shard_map/block_product/pallas_call | solution.py:420
  256.4 4.8 %copy.19 = bf16[8,16,128,128]{3,2,1,0:T(8,128)(2,1)} copy(bf16[8,16,128,128]{3,2,1,0:T(8,128)(2,1)} %block_product.1) | data formatting | bytes 8388608
  (3 shorter events, 0.0 us)
Async XLA Ops:
  0.0 0.8 copy-start

commit v4 on v3

v4 whole, which is shorter than its diff:
```python
import jax
import jax.numpy as jnp
from jax import lax
from jax.experimental import pallas as pl
from jax.experimental.pallas import tpu as pltpu
from jax.sharding import PartitionSpec as P

W = 24
LIST = 16
ROWS = 8
WINDOW = 2 * W + ROWS
MESH = pl.DeviceIdType.MESH
OWN, SIB, PAIR, PAIRF, YA, YB, YBF, DIN, OUT, RB, RBF, YP, YPF = range(13)
PARTS = 2
PIECES = ROWS * PARTS
SIZE = LIST // PARTS
DETOUR = 8 * PARTS
D_START = 9 * PARTS
PAIR_START = 3
RELAY_LAG = 12
RELAY_WAIT = 10
YP_LATE = 4
HOLD = 8
YA_HOLD = 16
YP_START = PIECES + 1
STEPS = max(PAIR_START + 2 * PIECES, YP_START + YP_LATE + PIECES, PAIR_START + RELAY_WAIT + 2 * PIECES)


def ring(side, i):
    return side * 3 + i * (1 - 2 * side)


def ring_of(group):
    slot = group // 4
    return ring(slot // 4, slot % 4)


class Place:
    def __init__(self):
        self.row = lax.axis_index("row")
        self.col = lax.axis_index("col")
        self.z, self.core = self.row // 2, self.row % 2
        self.y, self.x = self.col // 4, self.col % 4
        self.half = self.x // 2
        self.side = (self.x + self.half) % 2
        self.slot = self.side * 4 + ring(self.side, self.z)
        self.group = self.slot * 4 + self.y
        self.quarter = self.half * 2 + self.core
        self.start = self.group * 32 + self.quarter * 8

    def home(self, slot):
        side = slot // 4
        x = side + self.half * (3 - 2 * side)
        return (ring(side, slot % 4) * 2 + self.x % 2, self.y * 4 + x)

    def source(self, k):
        return (k, self.y * 4 + self.quarter)

    def member(self, group, core):
        slot = group // 4
        side = slot // 4
        x = side + self.half * (3 - 2 * side)
        return (ring(side, slot % 4) * 2 + core, (group % 4) * 4 + x)


def turn(i):
    i = i // 2
    return i + (i // 2) * (1 - 2 * (i % 2))


def arrival(z, j):
    i = j // PARTS
    return (((z - turn(i) + 4) % 4) * 2 + i % 2) * PARTS + j % PARTS


def kernel(index_ref, d_ref, h_ref, out_ref, window, dbuf, obuf, rbuf, send, recv):
    at = Place()
    row, core = at.row, at.core
    sibling = (at.row + 1 - 2 * core, at.col)
    pair = (at.row, at.y * 4 + 3 - at.x)
    heading = 1 - 2 * at.half
    facing = 2 * core - 1
    across = at.group + facing
    ahead = at.group + heading
    behind = at.group - heading
    has_across = (across >= 0) & (across < 32)
    has_ahead = (ahead >= 0) & (ahead < 32)
    has_behind = (behind >= 0) & (behind < 32)
    across_dev = at.member(across, 1 - core)
    ahead_dev = at.member(ahead, core)
    behind_dev = at.member(behind, core)
    stays = at.x % 2 == core
    def near(slot):
        return (slot >= 0) & (slot < 8)

    def flips(slot):
        return at.slot + slot == 7

    def pick(cond, a, b):
        return jnp.where(cond, a, b)

    seam_a = has_across & (at.y == 3 * core)
    held_a = seam_a & jnp.logical_not(flips(at.slot + facing))
    seam_ahead = has_ahead & (at.y == 3 - 3 * at.half)
    seam_behind = has_behind & (at.y == 3 * at.half)
    outer = core == at.half
    inner = core != at.half
    seam_b = seam_ahead & outer
    seam_in = seam_behind & outer
    flip_ahead = flips(at.slot + heading)
    flip_behind = flips(at.slot - heading)
    b_next = at.member(at.group + pick(flip_ahead, -3 * heading, 4 * heading), core)
    from_b = at.member(at.group + pick(flip_behind, -4 * heading, 3 * heading), core)
    turn_b = outer & (at.y == 3 * at.half) & flip_ahead
    relay_b = turn_b | (
        outer & (at.y == 3 - 3 * at.half) & near(at.slot - heading) & jnp.logical_not(flip_behind)
    )
    b_group = at.group + pick(turn_b, 3 * heading, -4 * heading)
    b_last = at.member(b_group, core)
    b_to = at.member(at.group + pick(turn_b, 4 * heading, -3 * heading), core)

    relays = DETOUR
    turns = DETOUR

    barrier = pltpu.get_barrier_semaphore()

    def greet(dev):
        pl.semaphore_signal(barrier, inc=1, device_id=dev, device_id_type=MESH)

    def greet_slot(i, _):
        @pl.when(jnp.logical_not(stays & (i == at.slot)))
        def _():
            greet(at.home(i))

        @pl.when(jnp.logical_not(stays & (i == row)))
        def _():
            greet(at.source(i))

        return 0

    lax.fori_loop(0, 8, greet_slot, 0)
    greet(sibling)
    greet(pair)
    pl.when(has_across)(lambda: greet(across_dev))
    pl.when(seam_b)(lambda: greet(b_next))
    pl.when(seam_in)(lambda: greet(from_b))
    pl.when(relay_b)(lambda: (greet(b_last), greet(b_to)) and None)
    pl.when(has_ahead)(lambda: greet(ahead_dev))
    pl.when(has_behind)(lambda: greet(behind_dev))
    count = (
        18
        - 2 * stays.astype(jnp.int32)
        + has_across.astype(jnp.int32)
        + seam_b.astype(jnp.int32)
        + seam_in.astype(jnp.int32)
        + 2 * relay_b.astype(jnp.int32)
        + has_ahead.astype(jnp.int32)
        + has_behind.astype(jnp.int32)
    )
    pl.semaphore_wait(barrier, count)

    def rows(w):
        return window.at[pl.ds(w * SIZE, SIZE)]

    def remote(src, dst, kind, s, r, dev, sent=None):
        return pltpu.make_async_remote_copy(
            src_ref=src,
            dst_ref=dst,
            send_sem=send.at[kind if sent is None else sent, s],
            recv_sem=recv.at[kind, r],
            device_id=dev,
            device_id_type=MESH,
        )

    one = PARTS
    own = W * one
    to_sib = own + 8 * one * facing
    at_pair = own + 16 * one * heading
    to_pair = own - 16 * one * heading
    pair_to_sib = own + 16 * one * heading + 8 * one * facing
    to_across = own - 24 * one * facing
    at_ahead = own - 16 * one * heading
    behind_to_sib = own - 16 * one * heading + 8 * one * facing
    across_to_pair = own + 24 * one * facing - 16 * one * heading
    from_pair = own - 16 * one * heading - 8 * one * facing

    def send_home(src_ref, buf, base, kind, i):
        part = i % PARTS
        i = i // PARTS
        side = at.side * (1 - 2 * (i % 2)) + i % 2
        slot = side * 4 + ring(side, (at.z + turn(i)) % 4)
        local = stays & (slot == at.slot)
        piece = row * PARTS + part
        src = src_ref.at[slot, pl.ds(part * SIZE, SIZE)]
        dst = buf.at[pl.ds((base + piece) * SIZE, SIZE)]

        @pl.when(local)
        def _():
            pltpu.make_async_copy(src, dst, recv.at[kind, piece]).start()

        @pl.when(jnp.logical_not(local))
        def _():
            remote(src, dst, kind, slot * PARTS + part, piece, at.home(slot)).start()

    def send_h(i, _):
        send_home(h_ref, window, own, OWN, i)
        return 0

    lax.fori_loop(0, PIECES, send_h, 0)

    def send_d(i, _):
        send_home(d_ref, dbuf, 0, DIN, PIECES - 1 - i)
        return 0

    def shared(k, seam):
        return (k % 2 == 1) | (seam & (k % 4 == 0))


    def relayed(i):
        return rbuf.at[pl.ds(i * SIZE, SIZE)]

    def arrived(ref, kind, k):
        pltpu.make_async_copy(ref, ref, recv.at[kind, k]).wait()

    def send_across(j):
        k = arrival(at.z, j)
        remote(rows(own + k), rows(to_across + k), YA, k, k, across_dev).start()

    def send_held_across(j, _):
        send_across(j)
        return 0

    def across_on(k):
        here = rows(own + 24 * one * facing + k)
        arrived(here, YA, k)
        remote(here, rows(across_to_pair + k), YBF, k, k, pair, YP).start()

    def send_ahead(j):
        k = arrival(at.z, j)
        here = rows(at_pair + k)
        around = seam_b & (j < turns)

        @pl.when(has_ahead & (outer | jnp.logical_not(shared(k, seam_ahead))) & jnp.logical_not(around))
        def _():
            remote(here, rows(at_ahead + k), YB, k, k, ahead_dev).start()

        @pl.when(around)
        def _():
            remote(here, relayed(j), RB, k, k, b_next, YB).start()

    def send_held(j, _):
        send_ahead(j)
        return 0

    def step(u, _):
        @pl.when(u < PIECES)
        def _():
            k = arrival(at.z, u)
            here = rows(own + k)
            arrived(here, OWN, k)
            remote(here, rows(to_pair + k), PAIR, k, k, pair).start()

            pl.when(has_across & (jnp.logical_not(held_a) | (u >= YA_HOLD)))(lambda: send_across(u))

            remote(here, rows(to_sib + k), SIB, k, k, sibling).start()

        @pl.when((u >= PAIR_START) & (u < PAIR_START + 2 * PIECES) & ((u - PAIR_START) % 2 == 0))
        def _():
            j = (u - PAIR_START) // 2
            k = arrival(at.z, j)
            here = rows(at_pair + k)
            arrived(here, PAIR, k)

            @pl.when(jnp.logical_not(seam_ahead) | (u >= HOLD))
            def _():
                send_ahead(j)

            remote(here, rows(pair_to_sib + k), PAIRF, k, k, sibling).start()

        @pl.when((u == YA_HOLD - 1) & held_a)
        def _():
            lax.fori_loop(0, YA_HOLD, send_held_across, 0)

        @pl.when((u == HOLD) & seam_ahead)
        def _():
            lax.fori_loop(0, (HOLD - PAIR_START + 1) // 2, send_held, 0)

        first = HOLD + RELAY_LAG
        slow = PAIR_START + RELAY_WAIT
        bend = first - slow
        early = (u >= first) & (u < first + bend)
        later = (u >= first + bend) & ((u - slow) % 2 == 0) & (u < slow + 2 * DETOUR)

        @pl.when((early | later) & relay_b)
        def _():
            j = pick(early, u - first, (u - slow) // 2)
            k = arrival(ring_of(b_group), j)
            here = relayed(j)
            arrived(here, RB, k)
            remote(here, rows(at_ahead + k), YB, k, k, b_to, RBF).start()

        turn_p = u - YP_START - pick(seam_a, YP_LATE, 0)

        @pl.when((turn_p >= 0) & (turn_p < PIECES) & inner & has_across)
        def _():
            k = arrival(ring_of(across), turn_p)
            pl.when(shared(k, seam_a))(lambda: across_on(k))

        @pl.when(u == D_START)
        def _():
            lax.fori_loop(0, PIECES, send_d, 0)

        return 0

    lax.fori_loop(0, STEPS, step, 0)

    def hand_on(j, _):
        k = arrival(ring_of(behind), j)

        @pl.when(outer | jnp.logical_not(shared(k, seam_behind)))
        def _():
            here = rows(at_ahead + k)
            arrived(here, YB, k)
            remote(here, rows(behind_to_sib + k), YBF, k, k, sibling).start()

        @pl.when(outer & shared(k, seam_behind))
        def _():
            here = rows(from_pair + k)
            arrived(here, YBF, k)
            remote(here, rows(at_ahead + k), YB, k, k, sibling, YPF).start()

        return 0

    @pl.when(has_behind)
    def _():
        lax.fori_loop(0, PIECES, hand_on, 0)

    zero = WINDOW * LIST
    window[zero] = jnp.zeros(window.shape[1:], window.dtype)

    def collect(k, _):
        one = rows(k)
        arrived(one, SIB, k)
        arrived(one, PAIRF, k)

        @pl.when(has_across & (outer | jnp.logical_not(shared(k, seam_a))))
        def _():
            arrived(one, YA, k)

        @pl.when(has_behind & (inner | jnp.logical_not(shared(k, seam_behind))))
        def _():
            arrived(one, YBF, k)

        @pl.when(has_behind & inner & shared(k, seam_behind))
        def _():
            arrived(one, YB, k)

        return 0

    lax.fori_loop(0, PIECES, collect, 0)

    def multiply(j, _):
        piece = arrival(at.z, PIECES - 1 - j)
        k = piece // PARTS
        part = piece % PARTS

        @pl.when(j % PARTS == 0)
        def _():
            for i in range(PARTS):
                arrived(rows(k * PARTS + i), DIN, k * PARTS + i)

        def columns(i, _):
            p = part * (SIZE // 2) + i
            total = jnp.zeros((128, 256), jnp.float32)
            for m in range(0, LIST, 2):
                left = jnp.concatenate([dbuf[k * LIST + m], dbuf[k * LIST + m + 1]], axis=1)
                base = (k * LIST + m) * LIST + 2 * p
                upper = jnp.concatenate([window[index_ref[base]], window[index_ref[base + 1]]], axis=1)
                lower = jnp.concatenate(
                    [window[index_ref[base + LIST]], window[index_ref[base + LIST + 1]]], axis=1
                )
                right = jnp.concatenate([upper, lower], axis=0)
                total = total + jnp.dot(left, right, preferred_element_type=jnp.float32)
            obuf[k * LIST + 2 * p] = total[:, :128].astype(obuf.dtype)
            obuf[k * LIST + 2 * p + 1] = total[:, 128:].astype(obuf.dtype)
            return 0

        lax.fori_loop(0, SIZE // 2, columns, 0)
        here = obuf.at[pl.ds(piece * SIZE, SIZE)]
        there = out_ref.at[at.slot, pl.ds(part * SIZE, SIZE)]
        place = at.slot * PARTS + part
        local = stays & (k == row)

        @pl.when(local)
        def _():
            pltpu.make_async_copy(here, there, recv.at[OUT, place]).start()

        @pl.when(jnp.logical_not(local))
        def _():
            remote(here, there, OUT, piece, place, at.source(k)).start()

        return 0

    lax.fori_loop(0, PIECES, multiply, 0)

    def finish(k, _):
        one = rows(k)

        def sent(kind):
            pltpu.make_async_copy(one, one, send.at[kind, k]).wait()

        @pl.when(jnp.logical_not(stays & (k // PARTS == at.slot)))
        def _():
            sent(OWN)
            sent(DIN)

        sent(SIB)
        sent(PAIR)
        sent(PAIRF)
        pl.when(has_across)(lambda: sent(YA))
        pl.when(has_ahead & (outer | jnp.logical_not(shared(k, seam_ahead))))(lambda: sent(YB))
        pl.when(has_behind & (outer | jnp.logical_not(shared(k, seam_behind))))(lambda: sent(YBF))
        pl.when(has_across & inner & shared(k, seam_a))(lambda: sent(YP))
        pl.when(has_behind & outer & shared(k, seam_behind))(lambda: sent(YPF))
        by_relay = relay_b & (k < 0)
        for j in range(PIECES):
            by_relay = by_relay | (relay_b & (j < relays) & (k == arrival(ring_of(b_group), j)))
        pl.when(by_relay)(lambda: sent(RBF))

        @pl.when(jnp.logical_not(stays & (k // PARTS == row)))
        def _():
            sent(OUT)

        arrived(out_ref.at[k // PARTS, pl.ds((k % PARTS) * SIZE, SIZE)], OUT, k)
        return 0

    lax.fori_loop(0, PIECES, finish, 0)


def match_index(density_cols, hamilton_cols):
    start = Place().start
    left = lax.dynamic_slice_in_dim(density_cols, start, ROWS, 0)
    right = jnp.take(hamilton_cols, left, axis=0)
    hit = right[:, :, None, :] == left[:, None, :, None]
    n = jnp.arange(LIST, dtype=jnp.int32)
    which = jnp.sum(jnp.where(hit, n, 0), axis=-1)
    block = (left - start + W)[:, :, None] * LIST + which
    return jnp.where(jnp.any(hit, axis=-1), block, WINDOW * LIST).reshape(-1).astype(jnp.int32)


def per_device(density_blocks, hamilton_blocks, density_cols, hamilton_cols):
    index = match_index(density_cols, hamilton_cols)
    block = density_blocks.shape[2:]
    kind = density_blocks.dtype
    return pl.pallas_call(
        kernel,
        out_shape=jax.ShapeDtypeStruct(density_blocks.shape, kind),
        in_specs=[
            pl.BlockSpec(memory_space=pltpu.SMEM),
            pl.BlockSpec(memory_space=pl.ANY),
            pl.BlockSpec(memory_space=pl.ANY),
        ],
        out_specs=pl.BlockSpec(memory_space=pl.ANY),
        scratch_shapes=[
            pltpu.VMEM((WINDOW * LIST + 1, *block), kind),
            pltpu.VMEM((ROWS * LIST, *block), kind),
            pltpu.VMEM((ROWS * LIST, *block), kind),
            pltpu.VMEM((PIECES * SIZE, *block), kind),
            pltpu.SemaphoreType.DMA((13, PIECES)),
            pltpu.SemaphoreType.DMA((13, PIECES)),
        ],
        compiler_params=pltpu.CompilerParams(
            collective_id=0, has_side_effects=True, vmem_limit_bytes=52 << 20
        ),
        name="block_product",
    )(index, density_blocks, hamilton_blocks)


def solution(mesh):
    return jax.shard_map(
        per_device,
        mesh=mesh,
        in_specs=(
            P(("row", "col"), None, None, None),
            P(("row", "col"), None, None, None),
            P(),
            P(),
        ),
        out_specs=P(("row", "col"), None, None, None),
        check_vma=False,
    )
```

time: 261 us -> 251 us (0.962)
  the two profiles are of different devices: /device:TPU:64 before, /device:TPU:62 now
where the time goes in v4:
time: 251 us
  Pallas kernels  238 us (95%)
  local copies, waits for them, and re-layouts  7.62 us (3%)
  other arithmetic  4.83 us (2%)
    pallas_call x1, Pallas kernels, per_device(): pl.pallas_call(kernel, out_shape=jax.ShapeDtypeStruct(density_blocks.shap...  238 us
    unnamed x5, local copies, waits for them, and re-layouts  6.74 us

profile of v4, /device:TPU:62, one launch (start us, length us, event | category | flops | bytes accessed | tf_op | source)
XLA Modules:
  0.0 250.7 jit_solution(16208828568816539010)
XLA Ops:
  0.0 0.0 copy-start
  0.0 0.8 copy-done
  0.8 0.1 constant_dynamic-slice_fusion
  0.9 0.1 copy.17
  1.0 0.1 reshape.20
  1.1 1.0 copy.16
  2.1 0.6 gather_fusion
  2.8 0.1 broadcast_select_fusion
  2.9 2.3 compare_reduce_fusion
  5.2 2.3 fusion
  7.5 0.1 add_select_fusion
  7.6 0.1 select_n.64.index_ref
  7.7 238.2 %block_product.1 = bf16[8,16,128,128]{3,2,1,0:T(8,128)(2,1)} custom-call(s32[2048]{0:T(1024)S(1)} %select_n.64.index_ref, bf16[8,16,128,128]{3,2,1,0:T(8,128)(2,1)} %d_ref.1, bf16[8,16,128,128]{3,2,1,0:T(8,128)(2,1)} %h_ref.1), custom_call_target="tpu_custom_call" | custom-call | tf_op jit(solution)/shard_map/block_product/pallas_call | solution.py:455
  245.9 4.8 %copy.19 = bf16[8,16,128,128]{3,2,1,0:T(8,128)(2,1)} copy(bf16[8,16,128,128]{3,2,1,0:T(8,128)(2,1)} %block_product.1) | data formatting | bytes 8388608
  (3 shorter events, 0.0 us)
Async XLA Ops:
  0.0 0.8 copy-start

commit v5 on v4

--- a/solution.py
+++ b/solution.py
@@ -16,10 +16,13 @@
 SIZE = LIST // PARTS
 DETOUR = 8 * PARTS
 D_START = 9 * PARTS
+D_BATCH = 4
+D_GAP = 4
 PAIR_START = 3
 RELAY_LAG = 12
 RELAY_WAIT = 10
 YP_LATE = 4
+SEAM_S = 4
 HOLD = 8
 YA_HOLD = 16
 YP_START = PIECES + 1
@@ -213,7 +216,7 @@
         return 0
 
     def shared(k, seam):
-        return (k % 2 == 1) | (seam & (k % 4 == 0))
+        return (k % 2 == 1) | (seam & (k % SEAM_S == 0))
 
 
     def relayed(i):
@@ -306,9 +309,11 @@
             k = arrival(ring_of(across), turn_p)
             pl.when(shared(k, seam_a))(lambda: across_on(k))
 
-        @pl.when(u == D_START)
-        def _():
-            lax.fori_loop(0, PIECES, send_d, 0)
+        batch = (u - D_START) // D_GAP
+
+        @pl.when((u >= D_START) & ((u - D_START) % D_GAP == 0) & (batch < PIECES // D_BATCH))
+        def _():
+            lax.fori_loop(batch * D_BATCH, (batch + 1) * D_BATCH, send_d, 0)
 
         return 0
 
@@ -374,12 +379,10 @@
             total = jnp.zeros((128, 256), jnp.float32)
             for m in range(0, LIST, 2):
                 left = jnp.concatenate([dbuf[k * LIST + m], dbuf[k * LIST + m + 1]], axis=1)
-                base = (k * LIST + m) * LIST + 2 * p
-                upper = jnp.concatenate([window[index_ref[base]], window[index_ref[base + 1]]], axis=1)
-                lower = jnp.concatenate(
-                    [window[index_ref[base + LIST]], window[index_ref[base + LIST + 1]]], axis=1
-                )
-                right = jnp.concatenate([upper, lower], axis=0)
+                met = [
+                    [window[index_ref[2 * p + q, k * LIST + m + i]] for q in (0, 1)] for i in (0, 1)
+                ]
+                right = jnp.concatenate([jnp.concatenate(one, axis=1) for one in met], axis=0)
                 total = total + jnp.dot(left, right, preferred_element_type=jnp.float32)
             obuf[k * LIST + 2 * p] = total[:, :128].astype(obuf.dtype)
             obuf[k * LIST + 2 * p + 1] = total[:, 128:].astype(obuf.dtype)
@@ -440,12 +443,13 @@
 def match_index(density_cols, hamilton_cols):
     start = Place().start
     left = lax.dynamic_slice_in_dim(density_cols, start, ROWS, 0)
-    right = jnp.take(hamilton_cols, left, axis=0)
-    hit = right[:, :, None, :] == left[:, None, :, None]
-    n = jnp.arange(LIST, dtype=jnp.int32)
-    which = jnp.sum(jnp.where(hit, n, 0), axis=-1)
-    block = (left - start + W)[:, :, None] * LIST + which
-    return jnp.where(jnp.any(hit, axis=-1), block, WINDOW * LIST).reshape(-1).astype(jnp.int32)
+    pairs = left.reshape(-1)
+    right = jnp.take(hamilton_cols, pairs, axis=0).T
+    wanted = jnp.broadcast_to(left.T[:, :, None], (LIST, ROWS, LIST)).reshape(LIST, -1)
+    n = jnp.arange(1, LIST + 1, dtype=jnp.int32)[:, None, None]
+    place = jnp.sum(jnp.where(right[:, None, :] == wanted[None, :, :], n, 0), axis=0)
+    block = (pairs - start + W)[None, :] * LIST + place - 1
+    return jnp.where(place > 0, block, WINDOW * LIST).astype(jnp.int32)
 
 
 def per_device(density_blocks, hamilton_blocks, density_cols, hamilton_cols):

time: 251 us -> 230 us (0.916)
  the two profiles are of different devices: /device:TPU:62 before, /device:TPU:64 now
where the time goes in v5:
time: 230 us
  Pallas kernels  222 us (97%)
  local copies, waits for them, and re-layouts  7.9 us (3%)
    pallas_call x1, Pallas kernels, per_device(): pl.pallas_call(kernel, out_shape=jax.ShapeDtypeStruct(density_blocks.shap...  222 us
    unnamed x4, local copies, waits for them, and re-layouts  6.66 us

profile of v5, /device:TPU:64, one launch (start us, length us, event | category | flops | bytes accessed | tf_op | source)
XLA Modules:
  0.0 230.2 jit_solution(11330216254992007901)
XLA Ops:
  0.0 0.0 copy-start
  0.0 0.8 copy-done
  0.8 0.1 fusion.1
  0.9 0.1 constant_dynamic-slice_fusion
  1.0 0.1 copy.9
  1.1 0.1 reshape.54
  1.1 0.1 reshape.55
  1.3 0.1 broadcast_in_dim.37
  1.3 0.1 eq.20
  1.4 1.0 copy.11
  2.5 0.6 gather_fusion
  3.1 0.1 select_bitcast_fusion
  3.2 0.1 copy.12
  3.3 0.1 select_reduce_fusion
  3.4 222.0 %block_product.1 = bf16[8,16,128,128]{3,2,1,0:T(8,128)(2,1)} custom-call(s32[16,128]{1,0:T(8,128)S(1)} %add_select_fusion.index_ref, bf16[8,16,128,128]{3,2,1,0:T(8,128)(2,1)} %d_ref.1, bf16[8,16,128,128]{3,2,1,0:T(8,128)(2,1)} %h_ref.1), custom_call_target="tpu_custom_call" | custom-call | tf_op jit(solution)/shard_map/block_product/pallas_call | solution.py:459
  225.4 4.8 %copy.14 = bf16[8,16,128,128]{3,2,1,0:T(8,128)(2,1)} copy(bf16[8,16,128,128]{3,2,1,0:T(8,128)(2,1)} %block_product.1) | data formatting | bytes 8388608
  (6 shorter events, 0.0 us)
Async XLA Ops:
  0.0 0.8 copy-start
